TPU v7x, 32 devices: a whole 2x2x4 slice. The times are simulated.
32 devices in a mesh: dp: 4 (over z), shard: 8 (over y, x, core).
Axes of the slice: x: 2, y: 2, z: 4, core: 2. Of those that a mesh axis runs over, the one named last changes fastest.
Arguments:
- conditions: bfloat16 [32, 3, 512, 512], P(('dp', 'shard')), may hold values from -6 to 6
- clean_latents: float32 [32, 4, 4096], P(('dp', 'shard')), may hold values from -6 to 6
- noise_field: float32 [32, 4, 4096], P(('dp', 'shard')), may hold values from -6 to 6
- timesteps: int32 [32], P(('dp', 'shard')), may hold values from 0 to 999
- text_states: bfloat16 [32, 77, 768], P(('dp', 'shard')), may hold values from -6 to 6
- text_lengths: int32 [32], P(('dp', 'shard')), may hold values from 5 to 77
- item_valid: int32 [32], P(('dp', 'shard')), may hold values 0 or 1
- unet_conv: bfloat16 [36, 320], replicated, may hold values from -1 to 1
- res_conv: bfloat16 [2, 2880, 320], replicated, may hold values from -0.109375 to 0.109375
- time_mlp: bfloat16 [320, 1280], replicated, may hold values from -0.3125 to 0.3125
- time_proj: bfloat16 [1280, 320], replicated, may hold values from -0.3125 to 0.3125
- query_proj: bfloat16 [320, 320], replicated, may hold values from -0.3125 to 0.3125
- keyvalue_proj: bfloat16 [768, 640], replicated, may hold values from -0.21875 to 0.21875
- output_proj: bfloat16 [320, 320], replicated, may hold values from -1.25 to 1.25
- geglu_in: bfloat16 [320, 2560], replicated, may hold values from -0.3125 to 0.3125
- geglu_out: bfloat16 [1280, 320], replicated, may hold values from -0.3125 to 0.3125
- velocity_proj: bfloat16 [320, 4], replicated, may hold values from -0.3125 to 0.3125
- adapter_in: float32 [1728, 320], P('shard'), may hold values from -0.15625 to 0.15625
- adapter_conv: float32 [2880, 320], P('shard'), may hold values from -0.109375 to 0.109375
- adapter_out: float32 [320, 320], P('shard'), may hold values from -0.3125 to 0.3125
- adapter_bias: float32 [960], P('shard'), may hold values from -0.25 to 0.25
- first_in: float32 [1728, 320], P('shard'), may hold values from -4.7683716e-06 to 4.7683716e-06
- first_conv: float32 [2880, 320], P('shard'), may hold values from -4.7683716e-06 to 4.7683716e-06
- first_out: float32 [320, 320], P('shard'), may hold values from -4.7683716e-06 to 4.7683716e-06
- first_bias: float32 [960], P('shard'), may hold values from -1.5258789e-05 to 1.5258789e-05
- second_in: float32 [1728, 320], P('shard'), may hold values from 6.337457e-14 to 2.5349829e-13
- second_conv: float32 [2880, 320], P('shard'), may hold values from 6.337457e-14 to 2.5349829e-13
- second_out: float32 [320, 320], P('shard'), may hold values from 6.337457e-14 to 2.5349829e-13
- second_bias: float32 [960], P('shard'), may hold values from 5.703711e-13 to 2.2814845e-12
Outputs:
- loss_sum: float32 [], replicated
- item_count: float32 [], replicated
- grad_norm: float32 [], replicated
- new_first_in: float32 [1728, 320], P('shard')
- new_first_conv: float32 [2880, 320], P('shard')
- new_first_out: float32 [320, 320], P('shard')
- new_first_bias: float32 [960], P('shard')
- new_second_in: float32 [1728, 320], P('shard')
- new_second_conv: float32 [2880, 320], P('shard')
- new_second_out: float32 [320, 320], P('shard')
- new_second_bias: float32 [960], P('shard')
- new_adapter_in: float32 [1728, 320], P('shard')
- new_adapter_conv: float32 [2880, 320], P('shard')
- new_adapter_out: float32 [320, 320], P('shard')
- new_adapter_bias: float32 [960], P('shard')
All inputs are finite; a program needn't handle non-finite values. No bound on the sum of `item_valid` on one device may be relied on, other than what follows from the above.
Results may differ from a plain program's by a relative error of at most 0.02.
Values may be sent and summed in bfloat16 or wider, within the bound.
No kernel may reach another device: no remote copies, remote signals or barrier semaphores. Data moves between devices by JAX's collectives and lax.ppermute only.
A program may use at most 320 MiB of HBM per device.

v0:
```python
import math

import jax
import jax.numpy as jnp
from jax import lax
from jax.sharding import PartitionSpec as P

HEADS = 8
GROUPS = 32
STEP = 10


LN_EPS = 1e-05
CLIP_MAX = 0.01
LEARN_RATE = 0.02
BETA_ONE = 0.9
BETA_TWO = 0.999
ADAM_EPS = 1e-08
WEIGHT_DECAY = 0.01


def plan():
    start = 0.00085**0.5
    final = 0.012**0.5
    places = jnp.arange(1000, dtype=jnp.int32).astype(jnp.float32)
    betas = (start + places * ((final - start) / 999.0)) ** 2
    return jnp.cumprod(1.0 - betas)


def lookup(table, index):
    places = jnp.arange(table.shape[0], dtype=jnp.int32)
    return jnp.sum(jnp.where(places == index, table, 0.0))


def shifted(field, tap_index, grid_side):
    chans = field.shape[-1]
    grid = field.reshape(grid_side, grid_side, chans)
    padded = jnp.pad(grid, ((1, 1), (1, 1), (0, 0)))
    row_off = tap_index // 3
    col_off = tap_index % 3
    return padded[row_off : row_off + grid_side, col_off : col_off + grid_side].reshape(
        grid_side * grid_side, chans
    )


def conv_three(field, kernel, grid_side):
    chans = field.shape[-1]
    total = jnp.zeros((field.shape[0], kernel.shape[1]), jnp.float32)
    for tap_index in range(9):
        part_rows = kernel[tap_index * chans : (tap_index + 1) * chans]
        total = total + jnp.dot(
            shifted(field, tap_index, grid_side), part_rows, preferred_element_type=jnp.float32
        )
    return total


def kernel_grad(field, grad_out, grid_side):
    pieces = []
    for tap_index in range(9):
        pieces.append(
            jnp.einsum(
                "pi,pj->ij",
                shifted(field, tap_index, grid_side),
                grad_out,
                preferred_element_type=jnp.float32,
            )
        )
    return jnp.concatenate(pieces, axis=0)


def input_grad(grad_out, kernel, grid_side):
    chans = kernel.shape[0] // 9
    total = jnp.zeros((grad_out.shape[0], chans), jnp.float32)
    for tap_index in range(9):
        part_rows = kernel[tap_index * chans : (tap_index + 1) * chans]
        back = jnp.einsum("pj,ij->pi", grad_out, part_rows, preferred_element_type=jnp.float32)
        total = total + shifted(back, 8 - tap_index, grid_side)
    return total


def group_stats(field):
    pixels, chans = field.shape
    grouped = field.reshape(pixels, GROUPS, chans // GROUPS)
    centered = grouped - jnp.mean(grouped, axis=(0, 2), keepdims=True)
    inv_std = lax.rsqrt(jnp.mean(centered * centered, axis=(0, 2), keepdims=True) + LN_EPS)
    return ((centered * inv_std).reshape(pixels, chans), inv_std)


def group_back(grad, normed, inv_std):
    pixels, chans = grad.shape
    grad_g = grad.reshape(pixels, GROUPS, chans // GROUPS)
    normed_g = normed.reshape(pixels, GROUPS, chans // GROUPS)
    result = inv_std * (
        grad_g
        - jnp.mean(grad_g, axis=(0, 2), keepdims=True)
        - normed_g * jnp.mean(grad_g * normed_g, axis=(0, 2), keepdims=True)
    )
    return result.reshape(pixels, chans)


def layer_stats(field):
    centered = field - jnp.mean(field, axis=-1, keepdims=True)
    inv_std = lax.rsqrt(jnp.mean(centered * centered, axis=-1, keepdims=True) + LN_EPS)
    return (centered * inv_std, inv_std)


def layer_back(grad, normed, inv_std):
    return inv_std * (
        grad
        - jnp.mean(grad, axis=-1, keepdims=True)
        - normed * jnp.mean(grad * normed, axis=-1, keepdims=True)
    )


def silu_slope(value):
    sigmoid_value = jax.nn.sigmoid(value)
    return sigmoid_value * (1.0 + value * (1.0 - sigmoid_value))


def gelu_slope(value):
    return 0.5 * (1.0 + lax.erf(value * 0.5**0.5)) + value * jnp.exp(-0.5 * value * value) * (
        2.0 * math.pi
    ) ** (-0.5)


def forward(weights, frozen, table, item):
    w_in, w_conv, w_out, biases = weights
    (
        unet_conv,
        res_conv,
        time_mlp,
        time_proj,
        query_proj,
        keyvalue_proj,
        output_proj,
        geglu_in,
        geglu_out,
        velocity_proj,
    ) = frozen
    image, clean, noise_field, tstep, text, length, item_flag = item
    grid_side = image.shape[-1] // 8
    width = w_in.shape[1]
    pixels = grid_side * grid_side
    head_dim = width // HEADS
    texts = text.shape[0]
    ff_width = geglu_out.shape[0]
    base = (
        image.reshape(3, grid_side, 8, grid_side, 8).transpose(1, 3, 0, 2, 4).reshape(pixels, 192)
    )
    first = conv_three(base, w_in, grid_side) + biases[:width].astype(jnp.float32)
    first_low = first.astype(jnp.bfloat16)
    inner = conv_three(first_low, w_conv, grid_side) + biases[width : 2 * width].astype(jnp.float32)
    mixed = jax.nn.silu(inner).astype(jnp.bfloat16)
    feature = (
        first
        + jnp.dot(mixed, w_out, preferred_element_type=jnp.float32)
        + biases[2 * width :].astype(jnp.float32)
    )
    half = width // 2
    freqs = jnp.exp(
        -math.log(10000.0) * jnp.arange(half, dtype=jnp.int32).astype(jnp.float32) / half
    )
    angles = tstep.astype(jnp.float32) * freqs
    emb = jnp.concatenate([jnp.cos(angles), jnp.sin(angles)])[None, :]
    temb = jnp.dot(emb.astype(jnp.bfloat16), time_mlp, preferred_element_type=jnp.float32)
    temb_add = jnp.dot(
        jax.nn.silu(temb).astype(jnp.bfloat16), time_proj, preferred_element_type=jnp.float32
    )
    abar = lookup(table, tstep)
    alpha_t = jnp.sqrt(abar)
    sigma_t = jnp.sqrt(1.0 - abar)
    noisy = (alpha_t * clean + sigma_t * noise_field).astype(jnp.bfloat16)
    h_zero = conv_three(noisy.T, unet_conv, grid_side) + feature
    group_one, inv_one = group_stats(h_zero)
    conv_one = (
        conv_three(jax.nn.silu(group_one).astype(jnp.bfloat16), res_conv[0], grid_side) + temb_add
    )
    group_two, inv_two = group_stats(conv_one)
    h_one = h_zero + conv_three(jax.nn.silu(group_two).astype(jnp.bfloat16), res_conv[1], grid_side)
    normed, inv_std = layer_stats(h_one)
    queries = jnp.dot(
        normed.astype(jnp.bfloat16), query_proj, preferred_element_type=jnp.float32
    ).astype(jnp.bfloat16)
    keyvals = jnp.dot(text, keyvalue_proj, preferred_element_type=jnp.float32).astype(jnp.bfloat16)
    query_heads = queries.reshape(pixels, HEADS, head_dim)
    key_heads = keyvals[:, :width].reshape(texts, HEADS, head_dim)
    value_heads = keyvals[:, width:].reshape(texts, HEADS, head_dim)
    scores = jnp.einsum(
        "phd,thd->hpt", query_heads, key_heads, preferred_element_type=jnp.float32
    ) * head_dim ** (-0.5)
    allowed = jnp.arange(texts, dtype=jnp.int32) < length
    scores = jnp.where(allowed[None, None, :], scores, -1000000000.0)
    top_score = jnp.max(scores, axis=-1, keepdims=True)
    expo = jnp.exp(scores - top_score)
    attend = expo / jnp.sum(expo, axis=-1, keepdims=True)
    heads_out = jnp.einsum(
        "hpt,thd->phd", attend.astype(jnp.bfloat16), value_heads, preferred_element_type=jnp.float32
    )
    heads_out = heads_out.reshape(pixels, width).astype(jnp.bfloat16)
    h_two = h_one + jnp.dot(heads_out, output_proj, preferred_element_type=jnp.float32)
    normed_two, inv_ff = layer_stats(h_two)
    proj = jnp.dot(normed_two.astype(jnp.bfloat16), geglu_in, preferred_element_type=jnp.float32)
    act = (proj[:, :ff_width] * jax.nn.gelu(proj[:, ff_width:], approximate=False)).astype(
        jnp.bfloat16
    )
    h_three = h_two + jnp.dot(act, geglu_out, preferred_element_type=jnp.float32)
    predicted = jnp.einsum(
        "pc,cl->lp", h_three.astype(jnp.bfloat16), velocity_proj, preferred_element_type=jnp.float32
    )
    target = alpha_t * noise_field - sigma_t * clean
    diff = predicted - target
    loss_term = item_flag * jnp.sum(diff * diff)
    saved = (
        base,
        first_low,
        inner,
        mixed,
        group_one,
        inv_one,
        group_two,
        inv_two,
        normed,
        inv_std,
        key_heads,
        value_heads,
        attend,
        normed_two,
        inv_ff,
        proj,
        diff,
        item_flag,
    )
    return (loss_term, saved)


def backward(weights, frozen, saved, count):
    w_in, w_conv, w_out, biases = weights
    (
        unet_conv,
        res_conv,
        time_mlp,
        time_proj,
        query_proj,
        keyvalue_proj,
        output_proj,
        geglu_in,
        geglu_out,
        velocity_proj,
    ) = frozen
    (
        base,
        first_low,
        inner,
        mixed,
        group_one,
        inv_one,
        group_two,
        inv_two,
        normed,
        inv_std,
        key_heads,
        value_heads,
        attend,
        normed_two,
        inv_ff,
        proj,
        diff,
        item_flag,
    ) = saved
    pixels = base.shape[0]
    grid_side = math.isqrt(pixels)
    width = w_in.shape[1]
    head_dim = key_heads.shape[-1]
    ff_width = geglu_out.shape[0]
    g_pred = (diff * (2.0 * item_flag / count)).astype(jnp.bfloat16)
    g_three = jnp.einsum("lp,cl->pc", g_pred, velocity_proj, preferred_element_type=jnp.float32)
    g_act = jnp.einsum(
        "pc,fc->pf", g_three.astype(jnp.bfloat16), geglu_out, preferred_element_type=jnp.float32
    )
    values_ff = proj[:, :ff_width]
    gates_ff = proj[:, ff_width:]
    g_proj = jnp.concatenate(
        [
            g_act * jax.nn.gelu(gates_ff, approximate=False),
            g_act * values_ff * gelu_slope(gates_ff),
        ],
        axis=-1,
    ).astype(jnp.bfloat16)
    g_normed_two = jnp.einsum("pf,cf->pc", g_proj, geglu_in, preferred_element_type=jnp.float32)
    g_two = g_three + layer_back(g_normed_two, normed_two, inv_ff)
    g_heads = jnp.einsum(
        "pc,dc->pd", g_two.astype(jnp.bfloat16), output_proj, preferred_element_type=jnp.float32
    )
    g_heads = g_heads.astype(jnp.bfloat16).reshape(pixels, key_heads.shape[1], head_dim)
    g_attend = jnp.einsum("phd,thd->hpt", g_heads, value_heads, preferred_element_type=jnp.float32)
    g_scores = attend * (g_attend - jnp.sum(attend * g_attend, axis=-1, keepdims=True))
    g_queries = jnp.einsum(
        "hpt,thd->phd", g_scores.astype(jnp.bfloat16), key_heads, preferred_element_type=jnp.float32
    ) * head_dim ** (-0.5)
    g_queries = g_queries.reshape(pixels, width).astype(jnp.bfloat16)
    g_normed = jnp.einsum("pd,cd->pc", g_queries, query_proj, preferred_element_type=jnp.float32)
    g_one = g_two + layer_back(g_normed, normed, inv_std)
    g_act_two = input_grad(g_one.astype(jnp.bfloat16), res_conv[1], grid_side)
    g_conv_one = group_back(g_act_two * silu_slope(group_two), group_two, inv_two).astype(
        jnp.bfloat16
    )
    g_act_one = input_grad(g_conv_one, res_conv[0], grid_side)
    g_hidden = g_one + group_back(g_act_one * silu_slope(group_one), group_one, inv_one)
    g_branch = g_hidden.astype(jnp.bfloat16)
    grad_out = jnp.einsum("pi,pj->ij", mixed, g_branch, preferred_element_type=jnp.float32)
    bias_out = jnp.sum(g_branch.astype(jnp.float32), axis=0)
    g_mixed = jnp.einsum("pj,ij->pi", g_branch, w_out, preferred_element_type=jnp.float32)
    g_inner = (g_mixed * silu_slope(inner)).astype(jnp.bfloat16)
    grad_conv = kernel_grad(first_low, g_inner, grid_side)
    bias_conv = jnp.sum(g_inner.astype(jnp.float32), axis=0)
    g_first = (g_hidden + input_grad(g_inner, w_conv, grid_side)).astype(jnp.bfloat16)
    grad_in = kernel_grad(base, g_first, grid_side)
    bias_in = jnp.sum(g_first.astype(jnp.float32), axis=0)
    grad_bias = jnp.concatenate([bias_in, bias_conv, bias_out])
    return (grad_in, grad_conv, grad_out, grad_bias)


def adamw(master, first, second, grad):
    new_first = BETA_ONE * first + (1.0 - BETA_ONE) * grad
    new_second = BETA_TWO * second + (1.0 - BETA_TWO) * grad * grad
    first_hat = new_first / (1.0 - BETA_ONE**STEP)
    second_hat = new_second / (1.0 - BETA_TWO**STEP)
    new_master = master - LEARN_RATE * (
        first_hat / (jnp.sqrt(second_hat) + ADAM_EPS) + WEIGHT_DECAY * master
    )
    return (new_first, new_second, new_master)


def per_device(
    conditions,
    clean_latents,
    noise_field,
    timesteps,
    text_states,
    text_lengths,
    item_valid,
    unet_conv,
    res_conv,
    time_mlp,
    time_proj,
    query_proj,
    keyvalue_proj,
    output_proj,
    geglu_in,
    geglu_out,
    velocity_proj,
    adapter_in,
    adapter_conv,
    adapter_out,
    adapter_bias,
    first_in,
    first_conv,
    first_out,
    first_bias,
    second_in,
    second_conv,
    second_out,
    second_bias,
):
    frozen = (
        unet_conv,
        res_conv,
        time_mlp,
        time_proj,
        query_proj,
        keyvalue_proj,
        output_proj,
        geglu_in,
        geglu_out,
        velocity_proj,
    )
    masters = (adapter_in, adapter_conv, adapter_out, adapter_bias)
    rounded = tuple((entry.astype(jnp.bfloat16) for entry in masters))
    weights = (
        lax.all_gather(rounded[0], "shard", axis=0, tiled=True),
        lax.all_gather(rounded[1], "shard", axis=0, tiled=True),
        lax.all_gather(rounded[2], "shard", axis=0, tiled=True),
        lax.all_gather(rounded[3], "shard", axis=0, tiled=True),
    )
    pixels = clean_latents.shape[-1]
    channels = clean_latents.shape[1]
    local_count = jnp.sum(item_valid).astype(jnp.float32) * (pixels * channels)
    count = jnp.maximum(lax.psum(local_count, ("dp", "shard")), 1.0)
    table = plan()
    item_index = 0
    item = (
        conditions[item_index],
        clean_latents[item_index],
        noise_field[item_index],
        timesteps[item_index],
        text_states[item_index],
        text_lengths[item_index],
        item_valid[item_index].astype(jnp.float32),
    )
    loss_term, saved = forward(weights, frozen, table, item)
    kept = [saved]
    grads = [jnp.zeros(entry.shape, jnp.float32) for entry in weights]
    item_index = 0
    terms = backward(weights, frozen, kept[item_index], count)
    grads = [terms[index] for index in range(4)]
    summed = (
        lax.psum(grads[0].astype(jnp.bfloat16), "dp").astype(jnp.float32),
        lax.psum(grads[1].astype(jnp.bfloat16), "dp").astype(jnp.float32),
        lax.psum(grads[2].astype(jnp.bfloat16), "dp").astype(jnp.float32),
        lax.psum(grads[3].astype(jnp.bfloat16), "dp").astype(jnp.float32),
    )
    owned = (
        lax.psum_scatter(
            summed[0].astype(jnp.bfloat16), "shard", scatter_dimension=0, tiled=True
        ).astype(jnp.float32),
        lax.psum_scatter(
            summed[1].astype(jnp.bfloat16), "shard", scatter_dimension=0, tiled=True
        ).astype(jnp.float32),
        lax.psum_scatter(
            summed[2].astype(jnp.bfloat16), "shard", scatter_dimension=0, tiled=True
        ).astype(jnp.float32),
        lax.psum_scatter(
            summed[3].astype(jnp.bfloat16), "shard", scatter_dimension=0, tiled=True
        ).astype(jnp.float32),
    )
    squares = jnp.zeros((), jnp.float32)
    for entry in owned:
        squares = squares + jnp.sum(entry * entry)
    totals = lax.psum((loss_term, squares), ("dp", "shard"))
    loss_sum = totals[0]
    grad_norm = jnp.sqrt(totals[1] / lax.axis_size("dp"))
    factor = jnp.minimum(1.0, CLIP_MAX / (grad_norm + 1e-06))
    firsts = (first_in, first_conv, first_out, first_bias)
    seconds = (second_in, second_conv, second_out, second_bias)
    results = [
        adamw(masters[index], firsts[index], seconds[index], owned[index] * factor)
        for index in range(4)
    ]
    return (
        loss_sum,
        count,
        grad_norm,
        results[0][0],
        results[1][0],
        results[2][0],
        results[3][0],
        results[0][1],
        results[1][1],
        results[2][1],
        results[3][1],
        results[0][2],
        results[1][2],
        results[2][2],
        results[3][2],
    )


def solution(mesh):
    placed = (
        P(("dp", "shard"), None, None, None),
        P(("dp", "shard"), None, None),
        P(("dp", "shard"), None, None),
        P(("dp", "shard")),
        P(("dp", "shard"), None, None),
        P(("dp", "shard")),
        P(("dp", "shard")),
        P(),
        P(),
        P(),
        P(),
        P(),
        P(),
        P(),
        P(),
        P(),
        P(),
        P("shard", None),
        P("shard", None),
        P("shard", None),
        P("shard"),
        P("shard", None),
        P("shard", None),
        P("shard", None),
        P("shard"),
        P("shard", None),
        P("shard", None),
        P("shard", None),
        P("shard"),
    )
    return jax.shard_map(
        per_device,
        mesh=mesh,
        in_specs=placed,
        out_specs=(
            P(),
            P(),
            P(),
            P("shard", None),
            P("shard", None),
            P("shard", None),
            P("shard"),
            P("shard", None),
            P("shard", None),
            P("shard", None),
            P("shard"),
            P("shard", None),
            P("shard", None),
            P("shard", None),
            P("shard"),
        ),
        check_vma=False,
    )
```

profile of v0, /device:TPU:0, one launch (start us, length us, event | category | flops | bytes accessed | tf_op | source)
XLA Modules:
  0.0 1324.1 jit_solution(126246906413068122)
XLA Ops:
  14.1 32.0 %reshape_squeeze.3 = bf16[3,64,8,64,8]{4,3,2,1,0:T(8,128)(2,1)} reshape(bf16[1,3,512,512]{3,2,1,0:T(8,128)(2,1)} %param.29) | data formatting | bytes 3145728 | tf_op jit(solution)/shard_map/reshape;squeeze | solution.py:148
  46.1 20.0 %copy.219 = bf16[64,64,3,8,8]{1,4,3,2,0:T(8,128)(2,1)} copy(bf16[64,64,3,8,8]{4,1,3,0,2:T(8,128)(2,1)} %bitcast.432) | data formatting | bytes 3145728 | tf_op jit(solution)/shard_map/transpose | solution.py:148
  66.2 22.2 %copy.225 = bf16[64,64,3,8,8]{1,0,4,3,2:T(8,128)(2,1)} copy(bf16[64,64,3,8,8]{4,1,3,0,2:T(8,128)(2,1)} %bitcast.433) | data formatting | bytes 3145728 | tf_op jit(solution)/shard_map/transpose | solution.py:148
  90.6 15.0 %all-reduce.30 = bf16[960]{0:T(1024)(128)(2,1)S(1)} all-reduce(bf16[960]{0:T(1024)(128)(2,1)S(1)} %dynamic-update-slice), channel_id=1, replica_groups=mesh['dp'=4,'shard'=8] {'shard'}, use_global_device_ids=true, to_apply=%add.30 | all-reduce | flops 960 | bytes 3840
  106.2 24.3 %pad_slice_fusion.48 = (bf16[64,64,192]{1,2,0:T(8,128)(2,1)}, bf16[64,64,192]{1,2,0:T(8,128)(2,1)}, bf16[64,64,192]{1,2,0:T(8,128)(2,1)}, bf16[64,64,192]{1,2,0:...) fusion(bf16[64,64,192]{1,2,0:T(8,128)(2,1)} %bitcast.503), kind=kLoop, calls=%fused_computation.244 | loop fusion | bytes 14155776 | tf_op jit(solution)/shard_map/slice | solution.py:41
  172.1 9.9 all_gather.15
  205.1 39.4 %psum.50 = f32[]{:T(128)} all-reduce(f32[]{:T(128)S(6)} %mul.546), channel_id=1, replica_groups=mesh['dp'=4,'shard'=8] {'dp','shard'}, use_global_device_ids=true, to_apply=%region_19.20 | all-reduce | flops 1 | bytes 8 | tf_op jit(solution)/shard_map/psum | solution.py:388
  283.6 22.0 %pad_slice_fusion.40 = (bf16[64,64,320]{2,1,0:T(8,128)(2,1)}, bf16[64,64,320]{2,1,0:T(8,128)(2,1)}, bf16[64,64,320]{2,1,0:T(8,128)(2,1)}, bf16[64,64,320]{2,1,0:...) fusion(bf16[64,64,320]{2,1,0:T(8,128)(2,1)} %bitcast.504), kind=kLoop, calls=%fused_computation.203 | loop fusion | bytes 23592960 | tf_op jit(solution)/shard_map/slice | solution.py:41
  354.9 16.9 %pad_slice_fusion.32 = (bf16[64,64,320]{2,1,0:T(8,128)(2,1)S(1)}, bf16[64,64,320]{2,1,0:T(8,128)(2,1)}, bf16[64,64,320]{2,1,0:T(8,128)(2,1)}, bf16[64,64,320]{2,...) fusion(bf16[64,64,320]{2,1,0:T(8,128)(2,1)} %bitcast.505), kind=kLoop, calls=%fused_computation.195 | loop fusion | bytes 23592960 | tf_op jit(solution)/shard_map/slice | solution.py:41
  395.5 6.5 multiply_convert_fusion.10
  406.5 18.4 %pad_slice_fusion.24 = (bf16[64,64,320]{2,1,0:T(8,128)(2,1)S(1)}, bf16[64,64,320]{2,1,0:T(8,128)(2,1)}, bf16[64,64,320]{2,1,0:T(8,128)(2,1)}, bf16[64,64,320]{2,...) fusion(bf16[64,64,320]{2,1,0:T(8,128)(2,1)} %bitcast.506), kind=kLoop, calls=%fused_computation.187 | loop fusion | bytes 23592960 | tf_op jit(solution)/shard_map/slice | solution.py:41
  454.6 9.6 fusion.266
  476.8 19.4 %fusion.66 = f32[4096,2560]{0,1:T(8,128)} fusion(bf16[320,2560]{1,0:T(8,128)(2,1)S(1)} %copy-done, f32[4096,320]{0,1:T(8,128)} %get-tuple-element.165, f32[4096]{0:T(1024)S(1)} %add_rsqrt_fusion, f32[4096]{0:T(1024)S(1)} %broadcast_multiply_fusion.4), kind=kOutput, calls=%fused_computation.179 | convolution fusion | flops 6714818560 | bytes 48857088 | tf_op jit(solution)/shard_map/dot_general | solution.py:202
  496.2 47.0 %fusion.2 = f32[4096,1280]{0,1:T(8,128)} fusion(f32[4096,2560]{0,1:T(8,128)} %fusion.66), kind=kLoop, calls=%fused_computation.4 | loop fusion | flops 335544320 | bytes 41943040 | tf_op jit(solution)/shard_map/mul | solution.py:203
  543.3 17.5 %multiply_reduce_fusion.9 = (f32[]{:T(128)}, f32[4,4096]{1,0:T(4,128)S(1)}) fusion(f32[1,4,4096]{2,1,0:T(4,128)S(1)} %copy-done.70, f32[]{:T(128)S(6)} %sqrt.22, f32[1,4,4096]{2,1,0:T(4,128)S(1)} %copy-done.72, f32[]{:T(128)S(6)} %sqrt.21, bf16[320,4]{0,1:T(4,128)(2,1)S(1)} %copy-done.92, f32[4096,320]{0,1:T(8,128)} %get-tuple-element.165, ...), kind=kOutput, calls=%fused_computation.404 | convolution fusion | flops 3379134464 | bytes 48204300 | tf_op jit(solution)/shard_map/pc,cl->lp/dot_general | solution.py:207
  564.0 34.8 %multiply_convert_fusion = (bf16[4096,1280]{0,1:T(8,128)(2,1)}, bf16[4096,1280]{0,1:T(8,128)(2,1)}) fusion(f32[4096,1280]{0,1:T(8,128)} %fusion.2, f32[4096,2560]{0,1:T(8,128)} %fusion.66, bf16[1280,320]{0,1:T(8,128)(2,1)S(1)} %copy-done.66, f32[4096,320]{0,1:T(8,128)} %fusion.229), kind=kOutput, calls=%fused_computation.15 | convolution fusion | flops 3424911360 | bytes 89948160 | tf_op jit(solution)/shard_map/pc,fc->pf/dot_general | solution.py:277
  598.9 14.1 %fusion.251 = (f32[4096]{0:T(1024)S(1)}, f32[4096]{0:T(1024)S(1)}, f32[4096,320]{0,1:T(8,128)}) fusion(f32[4096]{0:T(1024)S(1)} %add_rsqrt_fusion, f32[4096,320]{0,1:T(8,128)} %get-tuple-element.165, f32[4096]{0:T(1024)S(1)} %broadcast_multiply_fusion.4, bf16[320,2560]{1,0:T(8,128)(2,1)S(1)} %copy-done, bf16[4096,1280]{0,1:T(8,128)(2,1)} %get-tuple-element.106, ...), kind=kOutput, calls=%fused_computation.479 | convolution fusion | flops 6759374848 | bytes 33161216 | tf_op jit(solution)/shard_map/pf,cf->pc/dot_general | solution.py:289
  613.0 7.3 multiply_add_fusion.2
  621.8 9.2 multiply_reduce_fusion
  631.0 9.3 fusion.55
  644.5 9.1 fusion.259
  683.1 6.1 fusion.124
  704.1 6.2 copy.257
  710.3 6.2 pad_slice_fusion.17
  716.5 6.2 copy.256
  722.8 6.3 pad_slice_fusion.18
  729.1 6.2 copy.255
  735.3 6.4 pad_slice_fusion.19
  741.7 6.2 copy.254
  748.0 12.2 fusion.24
  760.2 6.4 copy.253
  766.6 13.8 %fusion.249 = (f32[320]{0:T(512)S(1)}, f32[320]{0:T(512)S(1)}, f32[4096,320]{0,1:T(8,128)}) fusion(f32[320]{0:T(512)S(1)} %copy-done.90, f32[4096,320]{0,1:T(8,128)} %get-tuple-element.159, f32[320]{0:T(512)S(1)} %copy-done.85, f32[4096,320]{0,1:T(8,128)} %copy.257, f32[4096,320]{0,1:T(8,128)} %copy.256, f32[4096,320]{0,1:T(8,128)} %copy.255, ...), kind=kOutput, calls=%fused_computation.477 | convolution fusion | flops 862453120 | bytes 39572480 | tf_op jit(solution)/shard_map/pj,ij->pi/dot_general | solution.py:76
  781.3 7.4 multiply_convert_fusion.9
  818.3 6.2 fusion.108
  839.3 6.2 copy.263
  845.5 6.2 pad_slice_fusion.9
  851.7 6.2 copy.262
  857.9 6.3 pad_slice_fusion.10
  864.2 6.2 copy.261
  870.4 6.4 pad_slice_fusion.11
  876.9 6.2 copy.260
  883.1 12.2 fusion.27
  895.4 6.4 copy.259
  901.8 13.7 %fusion.248 = (f32[320]{0:T(512)S(1)}, f32[320]{0:T(512)S(1)}, f32[4096,320]{0,1:T(8,128)}) fusion(f32[320]{0:T(512)S(1)} %copy-done.87, f32[4096,320]{0,1:T(8,128)} %get-tuple-element.157, f32[320]{0:T(512)S(1)} %copy-done.83, f32[4096,320]{0,1:T(8,128)} %copy.263, f32[4096,320]{0,1:T(8,128)} %copy.262, f32[4096,320]{0,1:T(8,128)} %copy.261, ...), kind=kOutput, calls=%fused_computation.476 | convolution fusion | flops 862453120 | bytes 39572480 | tf_op jit(solution)/shard_map/pj,ij->pi/dot_general | solution.py:76
  916.4 7.1 convert_reduce_fusion
  923.5 6.6 fusion.268
  990.7 6.2 copy.276
  996.9 6.2 pad_slice_fusion.1
  1003.1 6.2 copy.274
  1009.3 6.3 pad_slice_fusion.2
  1015.6 6.2 copy.272
  1021.9 6.4 pad_slice_fusion.3
  1028.3 6.2 copy.270
  1034.5 12.2 fusion.30
  1046.8 6.3 copy.268
  1053.0 11.9 fusion.269
  1087.9 6.5 convolution_convert_fusion.11
  1095.1 44.2 %all-reduce.41.cloned.1.call-done = bf16[2880,320]{0,1:T(8,128)(2,1)} async-done(((bf16[2880,320]{0,1:T(8,128)(2,1)}), bf16[2880,320]{0,1:T(8,128)(2,1)}) %all-reduce.41.cloned.1.call-update) | async-done | bytes 1843216
  1141.1 38.0 %reduce-scatter.8.cloned.1.call-done = bf16[216,320]{1,0:T(8,128)(2,1)} async-done(((bf16[1728,320]{1,0:T(8,128)(2,1)}), bf16[216,320]{1,0:T(8,128)(2,1)}) %reduce-scatter.8.cloned.1.call-update) | async-done | bytes 138256
  1180.9 12.7 all-reduce.34
  1193.6 21.8 %reduce-scatter.10.cloned.1.call-done = bf16[40,320]{1,0:T(8,128)(2,1)} async-done(((bf16[320,320]{1,0:T(8,128)(2,1)}), bf16[40,320]{1,0:T(8,128)(2,1)}) %reduce-scatter.10.cloned.1.call-update) | async-done | bytes 25616
  1215.4 19.8 %all-reduce.36 = (bf16[40,320]{1,0:T(8,128)(2,1)S(1)}, bf16[120]{0:T(256)(128)(2,1)S(1)}) all-reduce(bf16[40,320]{1,0:T(8,128)(2,1)} %reduce-scatter.10.cloned.1.call-done, bf16[120]{0:T(256)(128)(2,1)S(1)} %dynamic-slice.8), channel_id=1, replica_groups=mesh['dp'=4,'shard'=8] {'dp'}, use_global_device_ids=true, to_apply=%region_39.40 | all-reduce | flops 12920 | bytes 51680 | tf_op jit(solution)/shard_map/psum | solution.py:409
  1236.4 19.2 %all-reduce.43.cloned.1.call-done = (bf16[216,320]{1,0:T(8,128)(2,1)}, bf16[360,320]{0,1:T(8,128)(2,1)}) async-done(((bf16[216,320]{1,0:T(8,128)(2,1)}, bf16[360,320]{0,1:T(8,128)(2,1)}), (bf16[216,320]{1,0:T(8,128)(2,1)}, bf16[360,320]{0,1:T(8,128)(2,1)})) %all-reduce.43.cloned.1.call-update) | async-done | bytes 368656 | tf_op jit(solution)/shard_map/psum | solution.py:407
  1261.7 40.4 %all-reduce.35 = (f32[]{:T(128)}, f32[]{:T(128)}) all-reduce(f32[]{:T(128)S(6)} %mul.545, f32[]{:T(128)S(6)} %add.597), channel_id=1, replica_groups=mesh['dp'=4,'shard'=8] {'dp','shard'}, use_global_device_ids=true, to_apply=%region_18.19 | all-reduce | flops 2 | bytes 16 | tf_op jit(solution)/shard_map/psum | solution.py:429
  (459 shorter events, 429.1 us)
Async XLA Ops:
  7.2 469.6 %copy-start = (bf16[320,2560]{1,0:T(8,128)(2,1)S(1)}, bf16[320,2560]{1,0:T(8,128)(2,1)}, u32[]{:S(2)}) copy-start(bf16[320,2560]{1,0:T(8,128)(2,1)} %param.43) | copy-start | bytes 4915204
  7.2 247.9 %all-gather.5.cloned.1.call-start = ((), (), s32[]{:S(2)}) async-start(), calls=%async_computation.2 | async-start | bytes 1474560 | tf_op jit(solution)/shard_map/all_gather | solution.py:380
  9.0 296.6 %all-gather.7.cloned.1.call-start = ((), (), s32[]{:S(2)}) async-start(), calls=%async_computation.3 | async-start | bytes 2211840 | tf_op jit(solution)/shard_map/all_gather | solution.py:381
  10.9 1128.5 %all-reduce.41.cloned.1.call-start = ((), (), s32[]{:S(2)}) async-start(), calls=%async_computation.4 | async-start | bytes 3768320
  66.2 22.9 %copy-start.96 = (f32[120]{0:T(128)S(1)}, f32[120]{0:T(128)}, u32[]{:S(2)}) copy-start(f32[120]{0:T(128)} %param.49) | copy-start | bytes 1444
  66.2 22.9 %copy-start.94 = (u32[32]{0:T(128)S(1)}, u32[32]{0:T(128)}, u32[]{:S(2)}) copy-start(u32[32]{0:T(128)} %constant.254) | copy-start | bytes 388
  157.7 112.6 %copy-start.50 = (bf16[4096,192]{0,1:T(8,128)(2,1)}, bf16[4096,192]{0,1:T(8,128)(2,1)S(1)}, u32[]{:S(2)}) copy-start(bf16[4096,192]{0,1:T(8,128)(2,1)S(1)} %reshape.576) | copy-start | bytes 4718596
  162.9 9.2 copy-start.73
  162.9 19.1 %copy-start.69 = (f32[1,4,4096]{2,1,0:T(4,128)S(1)}, f32[1,4,4096]{2,1,0:T(4,128)}, u32[]{:S(2)}) copy-start(f32[1,4,4096]{2,1,0:T(4,128)} %param.30) | copy-start | bytes 196612
  162.9 19.1 %copy-start.71 = (f32[1,4,4096]{2,1,0:T(4,128)S(1)}, f32[1,4,4096]{2,1,0:T(4,128)}, u32[]{:S(2)}) copy-start(f32[1,4,4096]{2,1,0:T(4,128)} %param.31) | copy-start | bytes 196612
  250.1 4.0 copy-start.65
  313.2 17.0 %copy-start.9 = (bf16[2880,320]{0,1:T(8,128)(2,1)}, bf16[2880,320]{0,1:T(8,128)(2,1)S(1)}, u32[]{:S(2)}) copy-start(bf16[2880,320]{0,1:T(8,128)(2,1)S(1)} %reshape.638) | copy-start | bytes 5529604
  313.2 4.2 copy-start.24
  330.5 4.6 slice-start.4
  332.4 3.9 slice-start.5
  340.7 9.7 copy-start.82
  344.3 10.6 copy-start.86
  371.8 3.6 copy-start.29
  371.9 4.0 copy-start.31
  391.9 10.1 copy-start.84
  395.5 11.0 copy-start.89
  450.0 4.6 copy-start.2
  450.0 4.6 copy-start.61
  454.6 9.6 copy-start.80
  464.2 5.5 copy-start.3
  464.2 5.5 copy-start.56
  496.2 47.0 %copy-start.66 = (bf16[1280,320]{0,1:T(8,128)(2,1)S(1)}, bf16[1280,320]{0,1:T(8,128)(2,1)}, u32[]{:S(2)}) copy-start(bf16[1280,320]{0,1:T(8,128)(2,1)} %param.44) | copy-start | bytes 2457604
  496.2 47.1 %copy-start.70 = (f32[1,4,4096]{2,1,0:T(4,128)S(1)}, f32[1,4,4096]{2,1,0:T(4,128)}, u32[]{:S(2)}) copy-start(f32[1,4,4096]{2,1,0:T(4,128)} %param.30) | copy-start | bytes 196612
  496.2 47.1 %copy-start.72 = (f32[1,4,4096]{2,1,0:T(4,128)S(1)}, f32[1,4,4096]{2,1,0:T(4,128)}, u32[]{:S(2)}) copy-start(f32[1,4,4096]{2,1,0:T(4,128)} %param.31) | copy-start | bytes 196612
  496.2 47.1 %copy-start.92 = (bf16[320,4]{0,1:T(4,128)(2,1)S(1)}, bf16[320,4]{0,1:T(4,128)(2,1)}, u32[]{:S(2)}) copy-start(bf16[320,4]{0,1:T(4,128)(2,1)} %param.45) | copy-start | bytes 7684
  620.3 10.7 copy-start.4
  620.3 20.0 %slice-start = ((s8[5242880]{0:T(1024)(128)(4,1)}), s8[4194304]{0:T(1024)(128)(4,1)S(1)}, s32[]{:S(2)}) async-start(s8[5242880]{0:T(1024)(128)(4,1)} %bitcast.414), calls=%async_computation.8 | async-start | bytes 8388608
  621.8 18.5 %slice-start.1 = ((s8[5242880]{0:T(1024)(128)(4,1)}), s8[1048576]{0:T(1024)(128)(4,1)S(1)}, s32[]{:S(2)}) async-start(s8[5242880]{0:T(1024)(128)(4,1)} %bitcast.414), calls=%async_computation.9 | async-start | bytes 2097152
  631.0 9.3 copy-start.60
  631.0 9.4 copy-start.62
  631.0 9.4 copy-start.64
  760.2 6.4 copy-start.47
  760.2 6.4 copy-start.85
  760.2 6.4 copy-start.90
  895.4 6.4 copy-start.46
  895.4 6.4 copy-start.83
  895.4 6.4 copy-start.87
  916.4 7.1 copy-start.76
  923.5 6.6 copy-start.11
  923.5 6.6 copy-start.10
  961.6 4.8 copy-start.41
  1053.0 12.0 copy-start.45
  1053.0 13.4 %copy-start.40 = (bf16[64,64,192]{2,1,0:T(8,128)(2,1)S(1)}, bf16[64,64,192]{2,1,0:T(8,128)(2,1)}, u32[]{:S(2)}) copy-start(bf16[64,64,192]{2,1,0:T(8,128)(2,1)} %copy.222) | copy-start | bytes 4718596
  1065.0 7.1 copy-start.53
  1073.5 8.3 copy-start.33
  1077.8 101.3 %reduce-scatter.8.cloned.1.call-start = ((), (), s32[]{:S(2)}) async-start(), calls=%async_computation.5 | async-start | bytes 1492992
  1077.9 7.1 copy-start.49
  1077.9 7.1 copy-start.54
  1087.6 91.6 %copy-start.58 = (f32[216,320]{0,1:T(8,128)S(1)}, f32[216,320]{0,1:T(8,128)}, u32[]{:S(2)}) copy-start(f32[216,320]{0,1:T(8,128)} %param.46) | copy-start | bytes 829444
  1087.6 92.4 %copy-start.67 = (f32[216,320]{0,1:T(8,128)S(1)}, f32[216,320]{0,1:T(8,128)}, u32[]{:S(2)}) copy-start(f32[216,320]{0,1:T(8,128)} %param.54) | copy-start | bytes 829444
  1087.6 173.9 %copy-start.68 = (f32[216,320]{0,1:T(8,128)S(1)}, f32[216,320]{0,1:T(8,128)}, u32[]{:S(2)}) copy-start(f32[216,320]{0,1:T(8,128)} %param.50) | copy-start | bytes 829444
  1087.6 127.8 %reduce-scatter.10.cloned.1.call-start = ((), (), s32[]{:S(2)}) async-start(), calls=%async_computation.6 | async-start | bytes 276480
  1094.3 215.1 %copy-start.55 = (f32[360,320]{0,1:T(8,128)S(1)}, f32[360,320]{0,1:T(8,128)}, u32[]{:S(2)}) copy-start(f32[360,320]{0,1:T(8,128)} %param.47) | copy-start | bytes 1382404
  1094.4 161.2 %all-reduce.43.cloned.1.call-start = ((), (), s32[]{:S(2)}) async-start(), calls=%async_computation.7 | async-start | bytes 823296 | tf_op jit(solution)/shard_map/psum | solution.py:407
  1141.1 170.9 %copy-start.74 = (f32[40,320]{1,0:T(8,128)S(1)}, f32[40,320]{1,0:T(8,128)}, u32[]{:S(2)}) copy-start(f32[40,320]{1,0:T(8,128)} %param.48) | copy-start | bytes 153604
  1179.1 135.7 %copy-start.1 = (bf16[320,2560]{1,0:T(8,128)(2,1)S(1)}, bf16[320,2560]{1,0:T(8,128)(2,1)}, u32[]{:S(2)}) copy-start(bf16[320,2560]{1,0:T(8,128)(2,1)} %param.43) | copy-start | bytes 4915204
  1179.1 134.5 %copy-start.97 = (f32[120]{0:T(128)S(1)}, f32[120]{0:T(128)}, u32[]{:S(2)}) copy-start(f32[120]{0:T(128)} %param.49) | copy-start | bytes 1444
  1235.1 25.7 %copy-start.98 = (bf16[120]{0:T(256)(128)(2,1)}, bf16[120]{0:T(256)(128)(2,1)S(1)}, u32[]{:S(2)}) copy-start(bf16[120]{0:T(256)(128)(2,1)S(1)} %get-tuple-element.86) | copy-start | bytes 724
  1304.8 8.8 copy-start.99
  (51 other events, 112.7 us)
Sparse Core Ops, SparseCore 0:
  10.5 27.3 all-gather.4
  40.3 27.3 all-gather.6
  1077.9 61.3 all-reduce.40
  1142.5 36.5 reduce-scatter.7
  1182.6 32.7 reduce-scatter.9
  1218.2 37.3 all-reduce.42
where the time goes:
time: 1340 us; the launch traced here: 1320 us
  matrix products  449 us (34%)
  local copies, waits for them, and re-layouts  430 us (32%)
  other arithmetic  156 us (12%)
  blocking collectives  137 us (10%)
  waiting for transfers between devices  123 us (9%)
  between operations  28.4 us (2%)
    slice x25, local copies, waits for them, and re-layouts, shifted(): padded[row_off:row_off + grid_side, col_off:col_off + grid_side]  188 us
    dot_general x27, matrix products, input_grad(): jnp.einsum('pj,ij->pi', grad_out, part_rows, preferred_element_type=jnp.f...  163 us
    unnamed x9, waiting for transfers between devices  104 us
    dot_general x45, matrix products, conv_three(): jnp.dot(shifted(field, tap_index, grid_side), part_rows, preferred_elemen...  93.7 us
    reshape x21, local copies, waits for them, and re-layouts, shifted(): padded[row_off:row_off + grid_side, col_off:col_off + grid_side]  85.7 us
    mul x1, other arithmetic, forward(): jax.nn.gelu(proj[:, ff_width:], approximate=False)  47 us
    transpose x2, local copies, waits for them, and re-layouts, forward(): image.reshape(3, grid_side, 8, grid_side, 8).transpose(1, 3, 0, 2, 4)  42.2 us
    psum x1, blocking collectives, per_device(): totals = lax.psum((loss_term, squares), ('dp', 'shard'))  40.4 us
  transfers between devices with their start and end apart: 6, of which 4 were waited for; matrix products, arithmetic and copies ran while one was open for 18% of the time, Pallas kernels for 0%

commit v1 on v0

v1 whole, which is shorter than its diff:
```python
import math

import jax
import jax.numpy as jnp
import numpy as np
from jax import lax
from jax.experimental import pallas as pl
from jax.experimental.pallas import tpu as pltpu
from jax.sharding import PartitionSpec as P

HEADS = 8
GROUPS = 32
STEP = 10

LN_EPS = 1e-05
CLIP_MAX = 0.01
LEARN_RATE = 0.02
BETA_ONE = 0.9
BETA_TWO = 0.999
ADAM_EPS = 1e-08
WEIGHT_DECAY = 0.01

BF = jnp.bfloat16
F32 = jnp.float32

SIDE = 64
PIX = SIDE * SIDE
LANES = 128
HALO = LANES
WIDE = PIX + 2 * HALO
CH = 320
UNS = 192
FF = 1280
TXT = 80
KEYS = HEADS * TXT
NT = (((1,), (1,)), ((), ()))
TN = (((0,), (0,)), ((), ()))
VMEM_LIMIT = 60 * 2**20


def schedule():
    start = 0.00085**0.5
    final = 0.012**0.5
    betas = (start + np.arange(1000, dtype=np.float64) * ((final - start) / 999.0)) ** 2
    return np.cumprod(1.0 - betas).astype(np.float32)


def dot(a, b):
    return jnp.dot(a, b, preferred_element_type=F32)


def dot_nt(a, b):
    return lax.dot_general(a, b, NT, preferred_element_type=F32)


def al(x):
    return pl.multiple_of(x, LANES)


def tiles(width, body):
    def step(i, carry):
        body(al(i * width))
        return carry

    lax.fori_loop(0, PIX // width, step, 0)


def put(dst, value, p0, chans):
    width = value.shape[1]
    low = value.astype(BF)
    for q in range(width // LANES):
        mid = low[:, q * LANES : (q + 1) * LANES]
        lane = lax.broadcasted_iota(jnp.int32, mid.shape, 1) & (SIDE - 1)
        up = jnp.where(lane == 0, jnp.zeros((), BF), pltpu.roll(mid, 1, 1))
        down = jnp.where(lane == SIDE - 1, jnp.zeros((), BF), pltpu.roll(mid, LANES - 1, 1))
        at = pl.ds(al(p0 + HALO + q * LANES), LANES)
        dst[0:chans, at] = up
        dst[chans : 2 * chans, at] = mid
        dst[2 * chans : 3 * chans, at] = down


def ends(dst, rows):
    last = dst[0:rows, PIX : PIX + LANES]
    head = dst[0:rows, HALO : HALO + LANES]
    lane = lax.broadcasted_iota(jnp.int32, last.shape, 1)
    zero = jnp.zeros((), BF)
    dst[0:rows, 0:LANES] = jnp.where(lane >= SIDE, pltpu.roll(last, SIDE, 1), zero)
    dst[0:rows, PIX + HALO : PIX + HALO + LANES] = jnp.where(lane < SIDE, pltpu.roll(head, SIDE, 1), zero)


def conv(weight, src, p0, width, rows):
    parts = [src[0:rows, pl.ds(al(p0 + b * LANES), width)] for b in range(3)]
    return dot(weight, jnp.concatenate(parts, axis=0))


def lane_sum(value):
    total = value[:, 0:LANES]
    for q in range(1, value.shape[1] // LANES):
        total = total + value[:, q * LANES : (q + 1) * LANES]
    return total


def group_mean(gm, sums):
    spread = jnp.dot(gm, sums, precision=lax.Precision.HIGHEST, preferred_element_type=F32)
    return jnp.sum(spread, axis=1, keepdims=True) * (1.0 / (PIX * (CH // GROUPS)))


def silu_slope(y):
    s = jax.nn.sigmoid(y)
    return s * (1.0 + y * (1.0 - s))


def layer_stats(field):
    mean = jnp.mean(field, axis=0, keepdims=True)
    centered = field - mean
    inv = lax.rsqrt(jnp.mean(centered * centered, axis=0, keepdims=True) + LN_EPS)
    return centered * inv, inv


def layer_back(grad, normed, inv):
    return inv * (
        grad
        - jnp.mean(grad, axis=0, keepdims=True)
        - normed * jnp.mean(grad * normed, axis=0, keepdims=True)
    )


def prologue_kernel(
    scal, cond, perm, clean, noise, text, kvproj, wq, wo, wot, gout_w, vel, velt, emb, tmlp, tproj,
    base, nz, target, kq, kqb, vo, vob, gvt, gvl, temb,
    zs, us,
):
    alpha = scal[0]
    sigma = scal[1]
    lane = lax.broadcasted_iota(jnp.int32, (32, 8, LANES), 2)
    for c in range(3):
        zs[...] = lax.dot_general(cond[c], perm[...], TN, preferred_element_type=F32).reshape(64, 8, 512)
        for k in range(4):
            one = zs[0:32, :, k * LANES : (k + 1) * LANES]
            two = zs[32:64, :, k * LANES : (k + 1) * LANES]
            even = jnp.where(lane < SIDE, one, pltpu.roll(two, SIDE, 2))
            odd = jnp.where(lane < SIDE, pltpu.roll(one, SIDE, 2), two)
            for m in range(32):
                us[16 * k : 16 * k + 8, m * LANES : (m + 1) * LANES] = even[m]
                us[16 * k + 8 : 16 * k + 16, m * LANES : (m + 1) * LANES] = odd[m]
        base[64 * c : 64 * (c + 1), :] = us[...].astype(BF)
    noisy = (alpha * clean[...] + sigma * noise[...]).astype(BF).astype(F32)
    target[...] = alpha * noise[...] - sigma * clean[...]
    lane = lax.broadcasted_iota(jnp.int32, (8, LANES), 1)
    slot = lane & (SIDE - 1)
    cols = [noisy[:, m * LANES : (m + 1) * LANES] for m in range(32)]
    left = jnp.where(lane >= SIDE, pltpu.roll(cols[31], SIDE, 1), 0.0)
    right = jnp.where(lane < SIDE, pltpu.roll(cols[0], SIDE, 1), 0.0)
    cols = [left] + cols + [right]
    for m in range(34):
        up = jnp.where(slot == 0, 0.0, pltpu.roll(cols[m], 1, 1))
        down = jnp.where(slot == SIDE - 1, 0.0, pltpu.roll(cols[m], LANES - 1, 1))
        for a, part in enumerate((up, cols[m], down)):
            for b in range(3):
                at = m - b
                if 0 <= at < 32:
                    row = (b * 3 + a) * 8
                    if row < 64:
                        us[row : row + 8, at * LANES : (at + 1) * LANES] = part
                    else:
                        zs[at, :, 0:LANES] = part
    nz[0:64, :] = us[...].astype(BF)
    for m in range(32):
        tail = jnp.concatenate([zs[m, :, 0:LANES], jnp.zeros((8, LANES), F32)], axis=0)
        nz[64:80, m * LANES : (m + 1) * LANES] = tail.astype(BF)
    kv = dot(text[...], kvproj[...]).astype(BF)
    keys = kv[:, 0:CH]
    values = kv[:, CH : 2 * CH]
    head_dim = CH // HEADS
    head = lax.broadcasted_iota(jnp.int32, (TXT, CH), 1)
    own = [jnp.logical_and(head >= h * head_dim, head < (h + 1) * head_dim) for h in range(HEADS)]
    zero = jnp.zeros((), BF)
    kbd = jnp.concatenate([jnp.where(own[h], keys, zero) for h in range(HEADS)], axis=0)
    vbd = jnp.concatenate([jnp.where(own[h], values, zero) for h in range(HEADS)], axis=0)
    scale = head_dim ** (-0.5)
    kq[...] = (dot_nt(kbd, wq[...]) * scale).astype(BF)
    kqb[...] = (dot_nt(wq[...], kbd) * scale).astype(BF)
    vo[...] = dot_nt(wot[...], vbd).astype(BF)
    vob[...] = dot(vbd, wo[...]).astype(BF)
    fold_t = dot_nt(velt[...], gout_w[...])
    high_t = fold_t.astype(BF)
    gvt[...] = jnp.concatenate([high_t, (fold_t - high_t.astype(F32)).astype(BF)], axis=0)
    fold = dot(gout_w[...], vel[...])
    high = fold.astype(BF)
    low = (fold - high.astype(F32)).astype(BF)
    gvl[0:FF, :] = jnp.concatenate([high[:, 0:8], low[:, 0:8]], axis=1)
    gvl[FF : FF + CH, :] = vel[:, 0:16]
    hidden = dot(emb[...], tmlp[...])
    row = dot(jax.nn.silu(hidden).astype(BF), tproj[...])
    rows_i = lax.broadcasted_iota(jnp.int32, (CH, CH), 0)
    cols_i = lax.broadcasted_iota(jnp.int32, (CH, CH), 1)
    eye = jnp.where(rows_i == cols_i, 1.0, 0.0)
    full = jnp.concatenate([row] * 16, axis=0)
    temb[...] = lax.dot_general(eye, full, NT, precision=lax.Precision.HIGHEST, preferred_element_type=F32)


def prologue(scal, cond, perm, clean, noise, text, kvproj, wq, wo, wot, gout_w, vel, velt, emb, tmlp, tproj):
    vm = pl.BlockSpec(memory_space=pltpu.VMEM)
    sm = pl.BlockSpec(memory_space=pltpu.SMEM)
    shapes = [
        ((UNS, PIX), BF), ((80, PIX), BF), ((8, PIX), F32),
        ((KEYS, CH), BF), ((CH, KEYS), BF), ((CH, KEYS), BF), ((KEYS, CH), BF),
        ((16, FF), BF), ((FF + CH, 16), BF), ((CH, LANES), F32),
    ]
    return pl.pallas_call(
        prologue_kernel,
        out_shape=[jax.ShapeDtypeStruct(*s) for s in shapes],
        in_specs=[sm] + [vm] * 15,
        out_specs=[vm] * len(shapes),
        scratch_shapes=[pltpu.VMEM((64, 8, 512), F32), pltpu.VMEM((64, PIX), F32)],
        compiler_params=pltpu.CompilerParams(vmem_limit_bytes=VMEM_LIMIT),
        cost_estimate=pl.CostEstimate(flops=4_000_000_000, bytes_accessed=10_000_000, transcendentals=0),
        name="prologue",
    )(scal, cond, perm, clean, noise, text, kvproj, wq, wo, wot, gout_w, vel, velt, emb, tmlp, tproj)


TILE = 512
WIN = 1792
TILE_D = 256
CHUNK = 256


def main_kernel(
    scal, ilen, target, kq, kqb, vo, vob, gvt, gvl, velt, temb, bcols, gm, wou, wout,
    base, nz, win, wcf, wf, wb, git_hbm, gi_hbm,
    loss, gconv, gout, gbias, ginner_hbm, gh_hbm,
    sa, sb, hg, cu, y1s, y2s, flow, mx, ds, wbuf, git, gi, acc, stat, sems,
):
    flag = scal[2]
    fetch = [
        pltpu.make_async_copy(wcf, wbuf.at[0], sems.at[0]),
        pltpu.make_async_copy(wf.at[0], wbuf.at[1], sems.at[1]),
        pltpu.make_async_copy(wf.at[1], wbuf.at[0], sems.at[2]),
        pltpu.make_async_copy(wb.at[1], wbuf.at[1], sems.at[3]),
        pltpu.make_async_copy(wb.at[0], wbuf.at[0], sems.at[4]),
    ]
    get_git = pltpu.make_async_copy(git_hbm, git, sems.at[5])
    get_gi = pltpu.make_async_copy(gi_hbm, gi, sems.at[6])
    get_base = pltpu.make_async_copy(base, flow.at[0:UNS, :], sems.at[9])
    get_nz = pltpu.make_async_copy(nz, mx.at[CH : CH + 80, :], sems.at[10])
    get_win = pltpu.make_async_copy(win, wbuf.at[1, :, 0:WIN], sems.at[11])
    get_base.start()
    get_win.start()
    fetch[0].start()
    get_nz.start()
    get_git.start()
    get_gi.start()
    get_base.wait()

    def body(p0):
        put(sa, flow[0:UNS, pl.ds(p0, TILE)], p0, UNS)

    tiles(TILE, body)
    ends(sa, 3 * UNS)
    get_win.wait()

    def body(p0):
        at = pl.ds(p0, TILE)
        first = conv(wbuf[1, :, 0 : 9 * UNS], sa, p0, TILE, 3 * UNS) + bcols[:, 0:1]
        hg[:, at] = first
        low = first.astype(BF)
        flow[:, at] = low
        put(sb, low, p0, CH)

    tiles(TILE, body)
    ends(sb, 3 * CH)

    get_nz.wait()
    fetch[1].start()
    acc[...] = jnp.zeros_like(acc)
    fetch[0].wait()

    def body(p0):
        at = pl.ds(p0, TILE)
        inner = conv(wbuf[0], sb, p0, TILE, 3 * CH) + bcols[:, 1:2]
        s = jax.nn.sigmoid(inner)
        m = inner * s
        mx[0:CH, at] = m.astype(BF)
        ds[:, at] = (s + m * (1.0 - s)).astype(BF)
        h0 = hg[:, at] + dot(wou[...], mx[:, at]) + bcols[:, 2:3]
        hg[:, at] = h0
        acc[0] += lane_sum(h0)

    tiles(TILE, body)

    def norm_silu(field, store, dst, which):
        mean = group_mean(gm[...], acc[0])
        acc[1] = jnp.zeros_like(acc[1])

        def body(p0):
            centered = field[:, pl.ds(p0, TILE)] - mean
            acc[1] += lane_sum(centered * centered)

        tiles(TILE, body)
        inv = lax.rsqrt(group_mean(gm[...], acc[1]) + LN_EPS)
        stat[which] = jnp.broadcast_to(inv, (CH, LANES))

        def body(p0):
            at = pl.ds(p0, TILE)
            y = (field[:, at] - mean) * inv
            store[:, at] = y.astype(BF)
            put(dst, y * jax.nn.sigmoid(y), p0, CH)

        tiles(TILE, body)
        ends(dst, 3 * CH)
        acc[...] = jnp.zeros_like(acc)

    fetch[2].start()
    norm_silu(hg, y1s, sa, 0)
    fetch[1].wait()

    def body(p0):
        at = pl.ds(p0, TILE)
        c1 = conv(wbuf[1], sa, p0, TILE, 3 * CH) + temb[:, 0:1]
        cu[:, at] = c1
        acc[0] += lane_sum(c1)

    tiles(TILE, body)
    fetch[3].start()
    norm_silu(cu, y2s, sb, 1)

    fetch[2].wait()
    get_git.wait()
    get_gi.wait()
    loss[...] = jnp.zeros_like(loss)
    length = ilen[0]
    token = lax.broadcasted_iota(jnp.int32, (1, TXT, 1), 1)
    bias = jnp.where(token < length, 0.0, -1000000000.0)

    def body(p0):
        at = pl.ds(p0, TILE_D)
        h1 = hg[:, at] + conv(wbuf[0], sb, p0, TILE_D, 3 * CH)
        normed, inv = layer_stats(h1)
        s = dot(kq[...], normed.astype(BF)).reshape(HEADS, TXT, TILE_D) + bias
        e = jnp.exp(s - jnp.max(s, axis=1, keepdims=True))
        attend = e * (1.0 / jnp.sum(e, axis=1, keepdims=True))
        h2 = h1 + dot(vo[...], attend.reshape(KEYS, TILE_D).astype(BF))
        normed2, inv2 = layer_stats(h2)
        n2 = normed2.astype(BF)
        parts = []
        pred = dot(velt[...], h2.astype(BF))
        for f in range(0, FF, CHUNK):
            val = dot(git[f : f + CHUNK, :], n2)
            gate = dot(git[FF + f : FF + f + CHUNK, :], n2)
            phi = 0.5 + 0.5 * lax.erf(gate * 0.5**0.5)
            u = gate * phi
            slope = phi + gate * (jnp.exp(-0.5 * gate * gate) * (2.0 * math.pi) ** (-0.5))
            act = (val * u).astype(BF)
            both = dot(gvt[:, f : f + CHUNK], act)
            pred = pred + (both[0:8] + both[8:16])
            parts.append((u, val * slope))
        diff = pred - target[:, at]
        loss[...] += lane_sum(diff * diff) * flag
        gp = (diff * (2.0 * flag)).astype(BF)
        gp = jnp.concatenate([gp, gp], axis=0)
        pieces = []
        for k in (0, 1):
            for n, f in enumerate(range(0, FF, CHUNK)):
                g_act = dot(gvl[f : f + CHUNK, :], gp)
                pieces.append((g_act * parts[n][k]).astype(BF))
        g3 = dot(gvl[FF : FF + CH, :], gp)
        g_n2 = dot(gi[...], jnp.concatenate(pieces, axis=0))
        g2 = g3 + layer_back(g_n2, normed2, inv2)
        g_att = dot(vob[...], g2.astype(BF)).reshape(HEADS, TXT, TILE_D)
        prod = attend * g_att
        g_s = prod - attend * jnp.sum(prod, axis=1, keepdims=True)
        g_n = dot(kqb[...], g_s.reshape(KEYS, TILE_D).astype(BF))
        g1 = g2 + layer_back(g_n, normed, inv)
        hg[:, at] = g1
        put(sa, g1, p0, CH)

    tiles(TILE_D, body)
    ends(sa, 3 * CH)

    def conv_back(weight, src, ys):
        def body(p0):
            at = pl.ds(p0, TILE)
            y = ys[:, at].astype(F32)
            u = conv(weight[...], src, p0, TILE, 3 * CH) * silu_slope(y)
            cu[:, at] = u
            acc[0] += lane_sum(u)
            acc[1] += lane_sum(u * y)

        acc[...] = jnp.zeros_like(acc)
        tiles(TILE, body)
        return group_mean(gm[...], acc[0]), group_mean(gm[...], acc[1])

    fetch[4].start()
    fetch[3].wait()
    mean, cross = conv_back(wbuf.at[1], sa, y2s)
    inv = stat[1][:, 0:1]

    def body(p0):
        at = pl.ds(p0, TILE)
        put(sb, inv * (cu[:, at] - mean - y2s[:, at].astype(F32) * cross), p0, CH)

    tiles(TILE, body)
    ends(sb, 3 * CH)
    fetch[4].wait()
    mean, cross = conv_back(wbuf.at[0], sb, y1s)
    inv = stat[0][:, 0:1]

    gout[...] = jnp.zeros_like(gout)
    gbias[...] = jnp.zeros_like(gbias)

    def body(p0):
        at = pl.ds(p0, TILE)
        g0 = hg[:, at] + inv * (cu[:, at] - mean - y1s[:, at].astype(F32) * cross)
        hg[:, at] = g0
        branch = g0.astype(BF)
        g_inner = (dot(wout[...], branch) * ds[:, at].astype(F32)).astype(BF)
        put(sa, g_inner, p0, CH)
        gout[...] += dot_nt(mx[0:CH, at], branch)
        gbias[0] += lane_sum(g_inner.astype(F32))
        gbias[1] += lane_sum(branch.astype(F32))

    tiles(TILE, body)
    send_h = pltpu.make_async_copy(hg, gh_hbm, sems.at[7])
    send_g = pltpu.make_async_copy(sa.at[CH : 2 * CH, HALO : HALO + PIX], ginner_hbm, sems.at[8])
    send_h.start()
    send_g.start()
    ends(sa, 3 * CH)

    for b in range(3):
        grad = dot_nt(flow[...], sa[0 : 3 * CH, b * LANES : b * LANES + PIX])
        for a in range(3):
            t = 8 - 3 * a - b
            gconv[t * CH : (t + 1) * CH, :] = grad[:, a * CH : (a + 1) * CH].astype(BF)
    send_h.wait()
    send_g.wait()


def main_call(scal, ilen, *rest):
    vm = pl.BlockSpec(memory_space=pltpu.VMEM)
    sm = pl.BlockSpec(memory_space=pltpu.SMEM)
    hb = pl.BlockSpec(memory_space=pl.ANY)
    shapes = [
        ((8, LANES), F32), ((9 * CH, CH), BF), ((CH, CH), F32), ((2, CH, LANES), F32),
        ((CH, PIX), BF), ((CH, PIX), F32),
    ]
    return pl.pallas_call(
        main_kernel,
        out_shape=[jax.ShapeDtypeStruct(*s) for s in shapes],
        in_specs=[sm, sm] + [vm] * 13 + [hb] * 8,
        out_specs=[vm] * 4 + [hb] * 2,
        scratch_shapes=[
            pltpu.VMEM((3 * CH, WIDE), BF),
            pltpu.VMEM((3 * CH, WIDE), BF),
            pltpu.VMEM((CH, PIX), F32),
            pltpu.VMEM((CH, PIX), F32),
            pltpu.VMEM((CH, PIX), BF),
            pltpu.VMEM((CH, PIX), BF),
            pltpu.VMEM((CH, PIX), BF),
            pltpu.VMEM((CH + 80, PIX), BF),
            pltpu.VMEM((CH, PIX), BF),
            pltpu.VMEM((2, CH, 9 * CH), BF),
            pltpu.VMEM((2 * FF, CH), BF),
            pltpu.VMEM((CH, 2 * FF), BF),
            pltpu.VMEM((2, CH, LANES), F32),
            pltpu.VMEM((2, CH, LANES), F32),
            pltpu.SemaphoreType.DMA((12,)),
        ],
        compiler_params=pltpu.CompilerParams(vmem_limit_bytes=VMEM_LIMIT),
        cost_estimate=pl.CostEstimate(flops=80_000_000_000, bytes_accessed=40_000_000, transcendentals=0),
        name="main",
    )(scal, ilen, *rest)


def tail_kernel(ginner, base, wcb, gh_hbm, gin, gbias, sa, sb, gh, sem):
    fetch = pltpu.make_async_copy(gh_hbm, gh, sem)
    fetch.start()

    def body(p0):
        put(sa, ginner[:, pl.ds(p0, TILE)], p0, CH)

    tiles(TILE, body)
    ends(sa, 3 * CH)
    gbias[...] = jnp.zeros_like(gbias)
    fetch.wait()

    def body(p0):
        at = pl.ds(p0, TILE)
        g_first = (gh[:, at] + conv(wcb[...], sa, p0, TILE, 3 * CH)).astype(BF)
        put(sb, g_first, p0, CH)
        gbias[...] += lane_sum(g_first.astype(F32))

    tiles(TILE, body)
    ends(sb, 3 * CH)
    for b in range(3):
        grad = dot_nt(base[...], sb[0 : 3 * CH, b * LANES : b * LANES + PIX])
        for a in range(3):
            t = 8 - 3 * a - b
            gin[t * UNS : (t + 1) * UNS, :] = grad[:, a * CH : (a + 1) * CH].astype(BF)


def tail_call(ginner, base, wcb, gh):
    vm = pl.BlockSpec(memory_space=pltpu.VMEM)
    hb = pl.BlockSpec(memory_space=pl.ANY)
    return pl.pallas_call(
        tail_kernel,
        out_shape=[jax.ShapeDtypeStruct((9 * UNS, CH), BF), jax.ShapeDtypeStruct((CH, LANES), F32)],
        in_specs=[vm, vm, vm, hb],
        out_specs=[vm, vm],
        scratch_shapes=[
            pltpu.VMEM((3 * CH, WIDE), BF),
            pltpu.VMEM((3 * CH, WIDE), BF),
            pltpu.VMEM((CH, PIX), F32),
            pltpu.SemaphoreType.DMA(()),
        ],
        compiler_params=pltpu.CompilerParams(vmem_limit_bytes=VMEM_LIMIT),
        cost_estimate=pl.CostEstimate(flops=12_000_000_000, bytes_accessed=12_000_000, transcendentals=0),
        name="tail",
    )(ginner, base, wcb, gh)


def pixel_order(field):
    grid = field.reshape(4, SIDE, 2, SIDE // 2).transpose(0, 3, 2, 1).reshape(4, PIX)
    return jnp.pad(grid, ((0, 4), (0, 0)))


def forward_rows(weight, chans):
    return weight.reshape(3, 3, chans, CH).transpose(3, 1, 0, 2).reshape(CH, 9 * chans)


def backward_rows(weight):
    return weight.reshape(3, 3, CH, CH)[::-1, ::-1].transpose(2, 1, 0, 3).reshape(CH, 9 * CH)


def unshuffle_order():
    perm = np.zeros((512, 512), np.float32)
    for i in range(SIDE):
        for u in range(8):
            perm[i * 8 + u, u * SIDE + i] = 1.0
    return perm


def group_matrix():
    ids = np.arange(CH) // (CH // GROUPS)
    return (ids[:, None] == ids[None, :]).astype(np.float32)


def early(item, frozen):
    cond, clean, noise, tstep, text, length, flag = item
    unet_conv, res_conv, time_mlp, time_proj, wq, kvproj, wo, geglu_in, geglu_out, vel = frozen
    abar = jnp.asarray(schedule())[tstep]
    scal = jnp.stack([jnp.sqrt(abar), jnp.sqrt(1.0 - abar), flag, flag])
    half = CH // 2
    freqs = jnp.exp(-math.log(10000.0) * jnp.arange(half, dtype=jnp.int32).astype(F32) / half)
    angles = tstep.astype(F32) * freqs
    emb = jnp.concatenate([jnp.cos(angles), jnp.sin(angles)])[None, :].astype(BF)
    emb = jnp.broadcast_to(emb, (8, CH))
    perm = jnp.asarray(unshuffle_order(), BF)
    velt = jnp.pad(vel.T, ((0, 4), (0, 0)))
    velp = jnp.pad(vel, ((0, 0), (0, 12)))
    outs = prologue(
        scal, cond, perm, pixel_order(clean), pixel_order(noise), jnp.pad(text, ((0, TXT - text.shape[0]), (0, 0))),
        kvproj, wq, wo, wo.T, geglu_out, velp, velt, emb, time_mlp, time_proj,
    )
    wut = jnp.pad(unet_conv.reshape(3, 3, 4, CH).transpose(1, 0, 2, 3), ((0, 0), (0, 0), (0, 4), (0, 0)))
    wut = jnp.pad(wut.reshape(72, CH).T, ((0, 0), (0, 8)))
    wf = jnp.stack([forward_rows(res_conv[0], CH), forward_rows(res_conv[1], CH)])
    wb = jnp.stack([backward_rows(res_conv[0]), backward_rows(res_conv[1])])
    return scal, length.reshape(1), outs, velt, wut, wf, wb, geglu_in.T, geglu_in


def late(state, weights):
    scal, ilen, outs, velt, wut, wf, wb, git, gi = state
    base, nz, target, kq, kqb, vo, vob, gvt, gvl, temb = outs
    w_in, w_conv, w_out, biases = weights
    bcols = biases.astype(F32).reshape(3, CH).T
    wou = jnp.concatenate([w_out.T, wut], axis=1)
    gm = jnp.asarray(group_matrix())
    loss, gconv, gout, gbias, ginner, gh = main_call(
        scal, ilen, target, kq, kqb, vo, vob, gvt, gvl, velt, temb, bcols, gm, wou, w_out,
        base, nz, jnp.pad(forward_rows(w_in, UNS), ((0, 0), (0, WIN - 9 * UNS))), forward_rows(w_conv, CH), wf, wb, git, gi,
    )
    gin, gbin = tail_call(ginner, base, backward_rows(w_conv), gh)
    grad_bias = jnp.concatenate([jnp.sum(gbin, axis=1), jnp.sum(gbias, axis=2).reshape(-1)])
    return jnp.sum(loss), (gin, gconv, gout.astype(BF), grad_bias.astype(BF))


def adamw(master, first, second, grad):
    new_first = BETA_ONE * first + (1.0 - BETA_ONE) * grad
    new_second = BETA_TWO * second + (1.0 - BETA_TWO) * grad * grad
    first_hat = new_first / (1.0 - BETA_ONE**STEP)
    second_hat = new_second / (1.0 - BETA_TWO**STEP)
    new_master = master - LEARN_RATE * (
        first_hat / (jnp.sqrt(second_hat) + ADAM_EPS) + WEIGHT_DECAY * master
    )
    return (new_first, new_second, new_master)


def per_device(*args):
    conditions, clean, noise, tsteps, text, lengths, valid = args[:7]
    frozen = args[7:17]
    masters, firsts, seconds = args[17:21], args[21:25], args[25:29]
    weights = tuple(lax.all_gather(entry.astype(BF), "shard", axis=0, tiled=True) for entry in masters)
    item = (conditions[0], clean[0], noise[0], tsteps[0], text[0], lengths[0], valid[0].astype(F32))
    state = early(item, frozen)
    loss, grads = late(state, weights)
    owned = []
    for grad in grads:
        part = lax.psum_scatter(grad, "shard", scatter_dimension=0, tiled=True)
        owned.append(lax.psum(part, "dp").astype(F32))
    squares = jnp.zeros((), F32)
    for entry in owned:
        squares = squares + jnp.sum(entry * entry)
    pixels, channels = clean.shape[-1], clean.shape[1]
    local_count = jnp.sum(valid).astype(F32) * (pixels * channels)
    loss_sum, squares, count = lax.psum((loss, squares, local_count), ("dp", "shard"))
    count = jnp.maximum(count, 1.0)
    grad_norm = jnp.sqrt(squares / lax.axis_size("dp")) / count
    factor = jnp.minimum(1.0, CLIP_MAX / (grad_norm + 1e-06)) / count
    results = [adamw(masters[k], firsts[k], seconds[k], owned[k] * factor) for k in range(4)]
    return (loss_sum, count, grad_norm, *[results[k][n] for n in range(3) for k in range(4)])


def solution(mesh):
    both = ("dp", "shard")
    placed = (
        (P(both, None, None, None), P(both, None, None), P(both, None, None), P(both), P(both, None, None), P(both), P(both))
        + (P(),) * 10
        + (P("shard", None), P("shard", None), P("shard", None), P("shard")) * 3
    )
    return jax.shard_map(
        per_device,
        mesh=mesh,
        in_specs=placed,
        out_specs=(P(), P(), P()) + (P("shard", None), P("shard", None), P("shard", None), P("shard")) * 3,
        check_vma=False,
    )
```

time: 1340 us -> 580 us (0.43)
  matrix products: 449 us -> 0 us
  local copies, waits for them, and re-layouts: 430 us -> 89.7 us
  Pallas kernels: 0 us -> 223 us
  other arithmetic: 156 us -> 19.3 us
  blocking collectives: 137 us -> 97.8 us
    dot_general x108 -> x0, matrix products: 439 us -> none  [the longest x27 163 us: input_grad(): jnp.einsum('pj,ij->pi', grad_out, part_rows, preferred_element_type=jnp.f...]
    pallas_call x0 -> x3, Pallas kernels: none -> 223 us  [the longest x1 189 us: main_call(): pl.pallas_call(main_kernel, out_shape=[jax.ShapeDtypeStruct(*s) for s in...]
    slice x29 -> x1, local copies, waits for them, and re-layouts: 190 us -> 4.19 us  [early(): res_conv[0]]
    reshape x23 -> x8, local copies, waits for them, and re-layouts: 86.5 us -> 8.67 us  [the longest x2 5.75 us: forward_rows(): weight.reshape(3, 3, chans, CH).transpose(3, 1, 0, 2).reshape(CH, 9 * chans)]
    mul x2 -> x0, other arithmetic: 47.1 us -> none  [the longest x1 47 us: forward(): jax.nn.gelu(proj[:, ff_width:], approximate=False)]
    add x4 -> x0, other arithmetic: 44 us -> none  [the longest x3 36.7 us: input_grad(): total = total + shifted(back, 8 - tap_index, grid_side)]
    psum x3 -> x2, blocking collectives: 99.5 us -> 60.8 us  [the longest x1 41 us: per_device(): lax.psum((loss, squares, local_count), ('dp', 'shard'))]
    convert_element_type x9 -> x3, other arithmetic: 29.8 us -> 0.73 us  [the longest x1 0.72 us: late(): return (jnp.sum(loss), (gin, gconv, gout.astype(BF), grad_bias.astype(BF)))]
  transfers between devices with their start and end apart: 6 -> 6, of which waited for: 4 -> 4; matrix products, arithmetic and copies ran while one was open for 18% -> 14% of each run, Pallas kernels for 0% -> 2%
where the time goes in v1:
time: 580 us; the launch traced here: 574 us
  Pallas kernels  223 us (38%)
  waiting for transfers between devices  118 us (20%)
  blocking collectives  97.8 us (17%)
  local copies, waits for them, and re-layouts  89.7 us (15%)
  between operations  26 us (4%)
  other arithmetic  19.3 us (3%)
    pallas_call x1, Pallas kernels, main_call(): pl.pallas_call(main_kernel, out_shape=[jax.ShapeDtypeStruct(*s) for s in...  189 us
    unnamed x9, waiting for transfers between devices  98.7 us
    psum x1, blocking collectives, per_device(): lax.psum((loss, squares, local_count), ('dp', 'shard'))  41 us
    unnamed x2, blocking collectives  26.3 us
    pallas_call x1, Pallas kernels, tail_call(): pl.pallas_call(tail_kernel, out_shape=[jax.ShapeDtypeStruct((9 * UNS, CH)...  25.4 us
    unnamed x93, local copies, waits for them, and re-layouts  23.6 us
    psum x1, blocking collectives, per_device(): owned.append(lax.psum(part, 'dp').astype(F32))  19.8 us
    psum x1, waiting for transfers between devices, per_device(): owned.append(lax.psum(part, 'dp').astype(F32))  18.9 us
  transfers between devices with their start and end apart: 6, of which 4 were waited for; matrix products, arithmetic and copies ran while one was open for 14% of the time, Pallas kernels for 2%

profile of v1, /device:TPU:0, one launch (start us, length us, event | category | flops | bytes accessed | tf_op | source)
XLA Modules:
  0.0 573.7 jit_solution(12189212151270700131)
XLA Ops:
  7.2 1.8 convert_bitcast_fusion.1
  9.1 1.8 convert_bitcast_fusion
  11.6 1.3 dynamic_slice.3
  14.9 1.3 copy.121.gout_w
  16.2 1.3 copy.122.tproj
  18.6 0.7 pad.31.clean
  19.3 0.7 pad.32.noise
  20.0 0.9 copy.119
  21.6 0.6 pad.34.vel
  22.3 0.7 pad.33.text
  22.9 4.2 fusion.22
  27.1 3.3 copy.159
  30.4 1.6 reverse_bitcast_fusion.2
  32.0 4.2 copy.136
  36.2 4.1 copy.138
  40.3 4.0 copy.160
  44.3 3.3 reverse_bitcast_fusion.1
  47.5 4.2 copy.137
  51.8 4.0 copy.139
  55.8 1.6 copy.131
  57.4 4.4 copy.134
  61.8 1.6 copy.133
  63.5 4.2 copy.135
  67.7 10.7 %all_gather.13.wout = bf16[320,320]{1,0:T(8,128)(2,1)S(1)} all-gather(bf16[40,320]{1,0:T(8,128)(2,1)S(1)} %convert_element_type.69), channel_id=1, replica_groups=mesh['dp'=4,'shard'=8] {'shard'}, dimensions={0}, use_global_device_ids=true | all-gather | bytes 230400 | tf_op jit(solution)/shard_map/all_gather | solution.py:602
  78.5 0.9 copy.141.wou
  80.8 13.7 %all-reduce.8 = bf16[960]{0:T(1024)(128)(2,1)S(1)} all-reduce(bf16[960]{0:T(1024)(128)(2,1)S(1)} %dynamic-update-slice), channel_id=1, replica_groups=mesh['dp'=4,'shard'=8] {'shard'}, use_global_device_ids=true, to_apply=%add.8 | all-reduce | flops 960 | bytes 3840
  94.6 0.8 copy.123
  95.4 2.4 copy.140
  99.8 9.0 %prologue.1 = (bf16[192,4096]{1,0:T(8,128)(2,1)}, bf16[80,4096]{1,0:T(8,128)(2,1)}, f32[8,4096]{1,0:T(8,128)}, bf16[640,320]{1,0:T(8,128)(2,1)}, bf16[320,640]{1...) custom-call(f32[4]{0:T(128)} %pad_maximum_fusion.4.scal, ...), custom_call_target="tpu_custom_call" | custom-call | flops 4000000000 | bytes 10000000 | tf_op jit(solution)/shard_map/prologue/pallas_call | solution.py:210
  108.8 4.9 pad_maximum_fusion
  113.8 1.8 copy.125
  115.7 1.7 copy.127
  117.4 1.2 pad.38.win
  118.6 3.0 copy.128
  121.6 1.6 copy.129
  123.2 4.1 copy.142.wcf
  127.2 1.6 reverse_bitcast_fusion
  128.9 3.0 copy.143
  131.9 2.5 copy.144.wcb
  134.4 188.7 %main.1 = (f32[8,128]{1,0:T(8,128)}, bf16[2880,320]{1,0:T(8,128)(2,1)}, f32[320,320]{1,0:T(8,128)}, f32[2,320,128]{2,1,0:T(8,128)}, bf16[320,4096]{1,0:T(8,128)(2,1)}, /*index=5*/f32[320,4096]{1,0:T(8,128)}) custom-call(f32[4]{0:T(128)} %pad_maximum_fusion.4.scal, s32[1]{0:T(128)S(6)} %copy.167.ilen, f32[8,4096]{1,0:T(8,128)} %get-tuple-element.33.target, ...), custom_call_target="tpu_custom_call" | custom-call | flops 80000000000 | bytes 40000000 | tf_op jit(solution)/shard_map/main/pallas_call | solution.py:446
  323.0 25.4 %tail.1 = (bf16[1728,320]{1,0:T(8,128)(2,1)}, f32[320,128]{1,0:T(8,128)}) custom-call(bf16[320,4096]{1,0:T(8,128)(2,1)} %get-tuple-element.44.ginner, bf16[192,4096]{1,0:T(8,128)(2,1)} %get-tuple-element.41.base, bf16[320,2880]{1,0:T(8,128)(2,1)} %copy.144.wcb, f32[320,4096]{1,0:T(8,128)} %get-tuple-element.45.gh_hbm), custom_call_target="tpu_custom_call" | custom-call | flops 12000000000 | bytes 12000000 | tf_op jit(solution)/shard_map/tail/pallas_call | solution.py:504
  349.5 0.7 convert_element_type.74
  350.3 35.8 %reduce-scatter.10.cloned.1.call-done = bf16[216,320]{1,0:T(8,128)(2,1)} async-done(((bf16[1728,320]{1,0:T(8,128)(2,1)}), bf16[216,320]{1,0:T(8,128)(2,1)}) %reduce-scatter.10.cloned.1.call-update) | async-done | bytes 138256
  386.1 44.9 %reduce-scatter.12.cloned.1.call-done = bf16[360,320]{1,0:T(8,128)(2,1)} async-done(((bf16[2880,320]{1,0:T(8,128)(2,1)}), bf16[360,320]{1,0:T(8,128)(2,1)}) %reduce-scatter.12.cloned.1.call-update) | async-done | bytes 230416
  431.2 0.9 copy.150
  432.6 0.9 copy.145
  433.5 0.9 copy.147
  435.0 1.1 reduce_sum.71
  437.0 12.7 %all-reduce.12 = bf16[960]{0:T(1024)(128)(2,1)S(1)} all-reduce(bf16[960]{0:T(1024)(128)(2,1)S(1)} %pad_maximum_fusion.2), channel_id=5, replica_groups=mesh['dp'=4,'shard'=8] {'shard'}, use_global_device_ids=true, to_apply=%region_14.15.clone | all-reduce | flops 960 | bytes 3840
  449.8 17.4 %reduce-scatter.14.cloned.1.call-done = bf16[40,320]{1,0:T(8,128)(2,1)} async-done(((bf16[320,320]{1,0:T(8,128)(2,1)}), bf16[40,320]{1,0:T(8,128)(2,1)}) %reduce-scatter.14.cloned.1.call-update) | async-done | bytes 25616
  467.2 19.8 %all-reduce.14 = (bf16[40,320]{1,0:T(8,128)(2,1)S(1)}, bf16[120]{0:T(256)(128)(2,1)S(1)}) all-reduce(bf16[40,320]{1,0:T(8,128)(2,1)} %reduce-scatter.14.cloned.1.call-done, bf16[120]{0:T(256)(128)(2,1)S(1)} %dynamic-slice.8), channel_id=1, replica_groups=mesh['dp'=4,'shard'=8] {'dp'}, use_global_device_ids=true, to_apply=%region_10.11 | all-reduce | flops 12920 | bytes 51680 | tf_op jit(solution)/shard_map/psum | solution.py:609
  487.6 0.6 fusion.12
  488.2 18.9 %all-reduce.18.cloned.1.call-done = (bf16[216,320]{1,0:T(8,128)(2,1)}, bf16[360,320]{1,0:T(8,128)(2,1)}) async-done(((bf16[216,320]{1,0:T(8,128)(2,1)}, bf16[360,320]{1,0:T(8,128)(2,1)}), (bf16[216,320]{1,0:T(8,128)(2,1)}, bf16[360,320]{1,0:T(8,128)(2,1)})) %all-reduce.18.cloned.1.call-update) | async-done | bytes 368656 | tf_op jit(solution)/shard_map/psum | solution.py:609
  507.1 1.7 fusion.3
  508.8 1.6 fusion.7
  513.0 41.0 %all-reduce.13 = (f32[]{:T(128)}, f32[]{:T(128)}, f32[]{:T(128)}) all-reduce(f32[]{:T(128)} %reduce_sum.67, f32[]{:T(128)} %bitcast.32, f32[]{:T(128)S(6)} %add.116), channel_id=1, replica_groups=mesh['dp'=4,'shard'=8] {'dp','shard'}, use_global_device_ids=true, to_apply=%region_1.2 | all-reduce | flops 3 | bytes 24 | tf_op jit(solution)/shard_map/psum | solution.py:615
  555.5 1.4 multiply_subtract_fusion
  557.0 1.0 copy.154
  558.0 1.0 copy.156
  559.0 1.0 copy.158
  560.3 0.9 copy.153
  561.2 0.9 copy.155
  562.1 0.9 copy.157
  563.5 0.7 multiply_subtract_fusion.2
  (118 shorter events, 8.8 us)
Async XLA Ops:
  7.2 7.7 %copy-start.10 = (bf16[1280,320]{0,1:T(8,128)(2,1)S(1)}, bf16[1280,320]{0,1:T(8,128)(2,1)}, u32[]{:S(2)}) copy-start(bf16[1280,320]{0,1:T(8,128)(2,1)} %param.47) | copy-start | bytes 2457604
  7.2 9.0 %copy-start.11 = (bf16[1280,320]{0,1:T(8,128)(2,1)S(1)}, bf16[1280,320]{0,1:T(8,128)(2,1)}, u32[]{:S(2)}) copy-start(bf16[1280,320]{0,1:T(8,128)(2,1)} %param.42) | copy-start | bytes 2457604
  7.2 106.6 %all-gather.5.cloned.1.call-start = ((), (), s32[]{:S(2)}) async-start(), calls=%async_computation.3 | async-start | bytes 1474560 | tf_op jit(solution)/shard_map/all_gather | solution.py:602
  9.0 8.5 %copy-start.24 = (f32[1,4,4096]{2,1,0:T(4,128)S(1)}, f32[1,4,4096]{2,1,0:T(4,128)}, u32[]{:S(2)}) copy-start(f32[1,4,4096]{2,1,0:T(4,128)} %param.33) | copy-start | bytes 196612
  9.1 109.5 %all-gather.7.cloned.1.call-start = ((), (), s32[]{:S(2)}) async-start(), calls=%async_computation.4 | async-start | bytes 2211840 | tf_op jit(solution)/shard_map/all_gather | solution.py:602
  10.9 375.2 %reduce-scatter.10.cloned.1.call-start = ((), (), s32[]{:S(2)}) async-start(), calls=%async_computation.5 | async-start | bytes 1492992
  14.9 3.2 copy-start.25
  16.2 3.8 copy-start.20
  16.2 4.6 copy-start.29
  16.2 6.0 %copy-start.21 = (bf16[1,77,768]{2,1,0:T(8,128)(2,1)S(1)}, bf16[1,77,768]{2,1,0:T(8,128)(2,1)}, u32[]{:S(2)}) copy-start(bf16[1,77,768]{2,1,0:T(8,128)(2,1)} %param.36) | copy-start | bytes 354820
  57.4 4.4 copy-start
  63.4 4.2 copy-start.19
  63.4 4.2 copy-start.28
  63.4 15.9 %copy-start.32 = (f32[120]{0:T(128)S(1)}, f32[120]{0:T(128)}, u32[]{:S(2)}) copy-start(f32[120]{0:T(128)} %param.52) | copy-start | bytes 1444
  63.4 15.9 %copy-start.31 = (u32[32]{0:T(128)S(1)}, u32[32]{0:T(128)}, u32[]{:S(2)}) copy-start(u32[32]{0:T(128)} %constant.114) | copy-start | bytes 388
  63.5 32.0 %copy-start.4 = (bf16[320,2560]{1,0:T(8,128)(2,1)S(1)}, bf16[320,2560]{1,0:T(8,128)(2,1)}, u32[]{:S(2)}) copy-start(bf16[320,2560]{1,0:T(8,128)(2,1)} %gi_hbm.1) | copy-start | bytes 4915204
  78.4 19.4 %copy-start.9 = (bf16[320,320]{1,0:T(8,128)(2,1)}, bf16[320,320]{1,0:T(8,128)(2,1)S(1)}, u32[]{:S(2)}) copy-start(bf16[320,320]{1,0:T(8,128)(2,1)S(1)} %all_gather.13.wout) | copy-start | bytes 614404
  99.8 9.0 %copy-start.1 = (bf16[1,320,2880]{2,1,0:T(8,128)(2,1)S(1)}, bf16[1,320,2880]{2,1,0:T(8,128)(2,1)}, u32[]{:S(2)}) copy-start(bf16[1,320,2880]{2,1,0:T(8,128)(2,1)} %copy.138) | copy-start | bytes 5529604
  99.8 9.0 %copy-start.2 = (bf16[1,320,2880]{2,1,0:T(8,128)(2,1)S(1)}, bf16[1,320,2880]{2,1,0:T(8,128)(2,1)}, u32[]{:S(2)}) copy-start(bf16[1,320,2880]{2,1,0:T(8,128)(2,1)} %copy.139) | copy-start | bytes 5529604
  348.4 1.0 copy-start.15
  348.5 82.5 %copy-start.3 = (f32[360,320]{0,1:T(8,128)S(1)}, f32[360,320]{0,1:T(8,128)}, u32[]{:S(2)}) copy-start(f32[360,320]{0,1:T(8,128)} %param.50) | copy-start | bytes 1382404
  348.5 82.5 %reduce-scatter.12.cloned.1.call-start = ((), (), s32[]{:S(2)}) async-start(), calls=%async_computation.6 | async-start | bytes 2488320
  348.5 82.7 %copy-start.8 = (f32[216,320]{0,1:T(8,128)S(1)}, f32[216,320]{0,1:T(8,128)}, u32[]{:S(2)}) copy-start(f32[216,320]{0,1:T(8,128)} %param.49) | copy-start | bytes 829444
  348.5 83.6 %copy-start.13 = (f32[360,320]{0,1:T(8,128)S(1)}, f32[360,320]{0,1:T(8,128)}, u32[]{:S(2)}) copy-start(f32[360,320]{0,1:T(8,128)} %param.54) | copy-start | bytes 1382404
  349.1 83.3 %copy-start.14 = (f32[360,320]{0,1:T(8,128)S(1)}, f32[360,320]{0,1:T(8,128)}, u32[]{:S(2)}) copy-start(f32[360,320]{0,1:T(8,128)} %param.58) | copy-start | bytes 1382404
  349.1 118.1 %reduce-scatter.14.cloned.1.call-start = ((), (), s32[]{:S(2)}) async-start(), calls=%async_computation.7 | async-start | bytes 276480
  350.2 82.4 %copy-start.16 = (f32[216,320]{0,1:T(8,128)S(1)}, f32[216,320]{0,1:T(8,128)}, u32[]{:S(2)}) copy-start(f32[216,320]{0,1:T(8,128)} %param.53) | copy-start | bytes 829444
  350.2 156.9 %all-reduce.18.cloned.1.call-start = ((), (), s32[]{:S(2)}) async-start(), calls=%async_computation.8 | async-start | bytes 884736 | tf_op jit(solution)/shard_map/psum | solution.py:609
  431.0 2.5 copy-start.17
  431.2 4.9 copy-start.18
  431.2 5.1 copy-start.30
  487.0 68.5 %copy-start.22 = (bf16[40,320]{1,0:T(8,128)(2,1)}, bf16[40,320]{1,0:T(8,128)(2,1)S(1)}, u32[]{:S(2)}) copy-start(bf16[40,320]{1,0:T(8,128)(2,1)S(1)} %get-tuple-element.99) | copy-start | bytes 76804
  556.9 3.0 copy-start.5
  556.9 3.0 copy-start.6
  556.9 3.0 copy-start.7
  557.0 3.0 copy-start.12
  560.0 3.0 copy-start.33
  560.0 3.0 copy-start.34
  560.0 3.5 copy-start.23
  560.0 3.5 copy-start.26
  560.0 3.5 copy-start.27
Sparse Core Ops, SparseCore 0:
  9.9 27.2 all-gather.4
  39.7 27.3 all-gather.6
  348.6 37.4 reduce-scatter.9
  389.4 41.5 reduce-scatter.11
  434.4 32.7 reduce-scatter.13
  469.5 37.5 all-reduce.17
